TPU v7x, 32 devices: a whole 2x2x4 slice. The times are simulated.
32 devices in a mesh: slab: 8 (over z, x), chan: 4 (over y, core).
Axes of the slice: x: 2, y: 2, z: 4, core: 2. Of those that a mesh axis runs over, the one named last changes fastest.
Arguments:
- volume: bfloat16 [64, 8, 16, 128], P('chan', 'slab'), may hold values from -6 to 6
- kernel: bfloat16 [3, 3, 3, 64, 128], P(None, None, None, None, 'chan'), may hold values from -0.15625 to 0.15625
- bias: float32 [128], P('chan'), may hold values from -3 to 3
- out_grad: bfloat16 [128, 8, 16, 128], P('chan', 'slab'), may hold values from -6 to 6
Outputs:
- feature: bfloat16 [128, 8, 16, 128], P('chan', 'slab')
- input_grad: bfloat16 [64, 8, 16, 128], P('chan', 'slab')
- kernel_grad: float32 [3, 3, 3, 64, 128], P(None, None, None, None, 'chan')
- bias_grad: float32 [128], P('chan')
All inputs are finite; a program needn't handle non-finite values.
Results may differ from a plain program's by a relative error of at most 0.00105.
Values may be sent and summed in bfloat16 or wider, within the bound.
A program may use at most 64 MiB of HBM per device.

v0:
```python
import math

import jax
import jax.numpy as jnp
from jax import lax
from jax.sharding import PartitionSpec as P


def with_halo(value, sides, width):
    for axis, dim in sides:
        count, length = (lax.axis_size(axis), value.shape[dim])
        up = [(i, (i + 1) % count) for i in range(count - 1)]
        down = [(j, i) for i, j in up]
        last = lax.slice_in_dim(value, length - width, length, axis=dim)
        first = lax.slice_in_dim(value, 0, width, axis=dim)
        before = lax.ppermute(last, axis, up)
        after = lax.ppermute(first, axis, down)
        value = jnp.concatenate([before, value, after], axis=dim)
    return value


def conv_forward(source, kernel, depth_pad):
    result = lax.conv_general_dilated(
        source[None],
        kernel,
        (1, 1, 1),
        ((depth_pad, depth_pad), (1, 1), (1, 1)),
        dimension_numbers=("NCDHW", "DHWIO", "NCDHW"),
        preferred_element_type=jnp.float32,
    )
    return result[0]


def correlate(left, right):
    return lax.conv_general_dilated(
        left[:, None],
        right[:, None],
        (1, 1, 1),
        ((0, 0), (1, 1), (1, 1)),
        dimension_numbers=("NCDHW", "OIDHW", "NCDHW"),
        preferred_element_type=jnp.float32,
    )


def on_device(volume, kernel, bias, out_grad):
    in_local = volume.shape[0]
    plane_count = volume.shape[1]
    row_count = volume.shape[2]
    col_count = volume.shape[3]
    cell_total = plane_count * lax.axis_size("slab") * row_count * col_count
    joined = jnp.concatenate([volume, out_grad], axis=0)
    rimmed = with_halo(joined, (("slab", 1),), 1)
    volume_rim = rimmed[:in_local]
    grad_rim = rimmed[in_local:]
    gathered = lax.all_gather(volume_rim, "chan", axis=0, tiled=True)
    feature_sum = conv_forward(gathered, kernel, 0)
    kernel_local = jnp.transpose(correlate(gathered, out_grad), (2, 3, 4, 0, 1))
    feature = (feature_sum + bias[:, None, None, None]).astype(jnp.bfloat16)
    flipped = jnp.flip(kernel, (0, 1, 2))
    result = lax.conv_general_dilated(
        grad_rim[None],
        flipped,
        (1, 1, 1),
        ((0, 0), (1, 1), (1, 1)),
        dimension_numbers=("NCDHW", "DHWOI", "NCDHW"),
        preferred_element_type=jnp.float32,
    )
    input_grad = lax.psum_scatter(result[0], "chan", scatter_dimension=0, tiled=True).astype(
        jnp.bfloat16
    )
    bias_local = jnp.sum(out_grad.astype(jnp.float32), axis=(1, 2, 3))
    kernel_sum, bias_sum = lax.psum((kernel_local, bias_local), "slab")
    factor = 1.0 / math.sqrt(cell_total)
    return (feature, input_grad, kernel_sum * factor, bias_sum * factor)


def solution(mesh):
    in_specs = (
        P("chan", "slab", None, None),
        P(None, None, None, None, "chan"),
        P("chan"),
        P("chan", "slab", None, None),
    )
    out_specs = (
        P("chan", "slab", None, None),
        P("chan", "slab", None, None),
        P(None, None, None, None, "chan"),
        P("chan"),
    )
    return jax.shard_map(
        on_device, mesh=mesh, in_specs=in_specs, out_specs=out_specs, check_vma=False
    )
```

profile of v0, /device:TPU:0, one launch (start us, length us, event | category | flops | bytes accessed | tf_op | source)
XLA Modules:
  0.0 157.7 jit_solution(6914002378624086736)
XLA Ops:
  8.0 0.0 copy-start
  8.0 0.0 all-reduce.2.cloned.1.call-start
  8.1 0.9 constant_dynamic-update-slice_fusion.1
  9.0 0.9 constant_dynamic-update-slice_fusion
  9.9 4.9 %collective-permute-start = (bf16[48,1,16,128]{3,2,1,0:T(8,128)(2,1)S(1)}, bf16[48,1,16,128]{3,2,1,0:T(8,128)(2,1)S(1)}, u32[]{:S(2)}, u32[]{:S(2)}) collective-permute-start(bf16[48,1,16,128]{3,2,1,0:T(8,128)(2,1)S(1)} %constant_dynamic-update-slice_fusion), channel_id=1, source_target_pairs={{0,4},{4,8},{8,12},{12,16},{16,20},{20,24},{24,28},{1,5},{5,9},{9,... | collective-permute-start | bytes 589832 | tf_op jit(solution)/shard_map/ppermute | solution.py:16
  14.7 1.3 collective-permute-start.1
  16.0 2.6 %copy.34 = bf16[32,1,1,16,128]{0,1,4,3,2:T(2,128)(2,1)} copy(bf16[32,1,1,16,128]{4,3,0,2,1:T(8,128)(2,1)} %bitcast.41) | data formatting | bytes 262144 | tf_op jit(solution)/shard_map/broadcast_in_dim | solution.py:37
  18.6 1.2 convert_reduce_fusion
  19.8 22.8 %psum.15 = f32[32]{0:T(128)S(1)} all-reduce(f32[32]{0:T(128)S(1)} %convert_reduce_fusion), channel_id=1, replica_groups=mesh['slab'=8,'chan'=4] {'slab'}, use_global_device_ids=true, to_apply=%region_3.4 | all-reduce | flops 32 | bytes 256 | tf_op jit(solution)/shard_map/psum | solution.py:72
  42.6 0.0 collective-permute-done
  42.6 0.0 collective-permute-done.1
  42.7 8.6 %all_gather.3 = bf16[64,3,16,128]{3,2,1,0:T(8,128)(2,1)S(1)} all-gather(bf16[16,3,16,128]{3,2,1,0:T(8,128)(2,1)S(1)} %pad_maximum_fusion.2), channel_id=1, replica_groups=mesh['slab'=8,'chan'=4] {'chan'}, dimensions={0}, use_global_device_ids=true | all-gather | bytes 983040 | tf_op jit(solution)/shard_map/all_gather | solution.py:55
  51.3 1.2 copy.36
  52.5 0.3 pad.2
  52.8 0.0 copy-start.3
  52.8 0.4 copy.30
  53.3 0.1 slice.14
  53.3 0.0 copy-done
  53.4 0.2 copy-done.3
  53.5 2.1 %fusion.19 = f32[1,16,8,17,64]{4,2,3,1,0:T(8,128)S(1)} fusion(bf16[3,3,3,64,32]{3,4,2,1,0:T(8,128)(2,1)S(1)} %copy-done, bf16[32,3,16,1,7,2]{0,4,5,2,1,3:T(8,128)(2,1)S(1)} %slice.14, bf16[32,3,16,1,8,17]{0,4,5,2,1,3:T(8,128)(2,1)S(1)} %copy.30, pred[8,17]{0,1:T(8,128)(4,1)S(1)} %copy-done.3), kind=kOutput, calls=%fused_computation.17 | convolution fusion | flops 232161280 | bytes 1128584 | tf_op jit(solution)/shard_map/conv_general_dilated | solution.py:60
  55.6 0.2 copy.31
  55.8 0.0 copy-start.1
  55.8 3.7 %copy.33 = bf16[64,1,3,16,128]{0,1,4,3,2:T(2,128)(2,1)} copy(bf16[64,1,3,16,128]{4,3,2,0,1:T(8,128)(2,1)S(1)} %bitcast.34) | data formatting | bytes 1572864 | tf_op jit(solution)/shard_map/broadcast_in_dim | solution.py:36
  59.5 0.0 copy-done.1
  59.5 19.1 %fusion.32 = f32[3,3,3,64,32]{3,4,2,1,0:T(8,128)} fusion(bf16[64,1,3,16,128]{0,1,4,3,2:T(2,128)(2,1)} %copy.33, bf16[32,1,1,16,128]{0,1,4,3,2:T(2,128)(2,1)S(1)} %copy-done.1), kind=kOutput, calls=%fused_computation.38 | convolution fusion | flops 215924736 | bytes 1138688 | tf_op jit(solution)/shard_map/transpose | solution.py:57
  78.6 0.0 all-reduce.2.cloned.1.call-update
  78.6 0.0 reduce-scatter.2.cloned.1.call-start
  78.6 0.1 slice_bitcast_fusion
  78.7 1.3 copy.32
  80.0 0.0 reduce-scatter.2.cloned.1.call-update
  80.1 0.5 broadcast_multiply_fusion.1
  80.6 1.3 copy.24
  81.9 0.3 pad
  82.2 0.4 copy.26
  82.7 0.1 slice.12
  82.7 4.2 %fusion.16 = f32[1,16,8,17,32]{4,2,3,1,0:T(8,128)S(1)} fusion(bf16[3,3,3,64,32]{3,4,2,1,0:T(8,128)(2,1)S(1)} %copy-done, bf16[64,3,16,1,7,2]{0,4,5,2,1,3:T(8,128)(2,1)S(1)} %slice.12, bf16[64,3,16,1,8,17]{0,4,5,2,1,3:T(8,128)(2,1)S(1)} %copy.26, pred[8,17]{0,1:T(8,128)(4,1)S(1)} %copy-done.3), kind=kOutput, calls=%fused_computation.16 | convolution fusion | flops 233492480 | bytes 1310856 | tf_op jit(solution)/shard_map/conv_general_dilated | solution.py:23
  87.0 0.0 copy-start.2
  87.0 0.2 copy.27
  87.2 0.4 copy-done.2
  87.6 0.1 fusion.23
  87.7 1.2 copy.35
  88.9 58.0 %all-reduce.2.cloned.1.call-done = f32[3,3,3,64,32]{3,4,2,1,0:T(8,128)} async-done(((f32[3,3,3,64,32]{3,4,2,1,0:T(8,128)}), f32[3,3,3,64,32]{3,4,2,1,0:T(8,128)}) %all-reduce.2.cloned.1.call-update) | async-done | bytes 221200 | tf_op jit(solution)/shard_map/psum | solution.py:72
  146.9 1.8 %broadcast_multiply_fusion = f32[3,3,3,64,32]{3,4,2,1,0:T(8,128)} fusion(f32[3,3,3,64,32]{3,4,2,1,0:T(8,128)} %all-reduce.2.cloned.1.call-done), kind=kLoop, calls=%fused_computation.27 | loop fusion | flops 55296 | bytes 442368 | tf_op jit(solution)/shard_map/mul | solution.py:74
  148.7 0.0 reduce-scatter.2.cloned.1.call-done
  148.7 1.5 convert_element_type.18
  (2 shorter events, 0.1 us)
Async XLA Ops:
  8.0 45.4 %copy-start = (bf16[3,3,3,64,32]{3,4,2,1,0:T(8,128)(2,1)S(1)}, bf16[3,3,3,64,32]{3,4,2,1,0:T(8,128)(2,1)}, u32[]{:S(2)}) copy-start(bf16[3,3,3,64,32]{3,4,2,1,0:T(8,128)(2,1)} %param.5) | copy-start | bytes 331780
  8.0 138.9 %all-reduce.2.cloned.1.call-start = ((), (), s32[]{:S(2)}) async-start(), calls=%async_computation.2 | async-start | bytes 884736 | tf_op jit(solution)/shard_map/psum | solution.py:72
  9.9 32.8 %collective-permute-start = (bf16[48,1,16,128]{3,2,1,0:T(8,128)(2,1)S(1)}, bf16[48,1,16,128]{3,2,1,0:T(8,128)(2,1)S(1)}, u32[]{:S(2)}, u32[]{:S(2)}) collective-permute-start(bf16[48,1,16,128]{3,2,1,0:T(8,128)(2,1)S(1)} %constant_dynamic-update-slice_fusion), channel_id=1, source_target_pairs={{0,4},{4,8},{8,12},{12,16},{16,20},{20,24},{24,28},{1,5},{5,9},{9,... | collective-permute-start | bytes 589832 | tf_op jit(solution)/shard_map/ppermute | solution.py:16
  14.7 27.9 %collective-permute-start.1 = (bf16[48,1,16,128]{3,2,1,0:T(8,128)(2,1)S(1)}, bf16[48,1,16,128]{3,2,1,0:T(8,128)(2,1)S(1)}, u32[]{:S(2)}, u32[]{:S(2)}) collective-permute-start(bf16[48,1,16,128]{3,2,1,0:T(8,128)(2,1)S(1)} %constant_dynamic-update-slice_fusion), channel_id=1, source_target_pairs={{4,0},{8,4},{12,8},{16,12},{20,16},{24,20},{28,24},{5,1},{9,5},{13... | collective-permute-start | bytes 589832 | tf_op jit(solution)/shard_map/ppermute | solution.py:17
  52.8 0.7 copy-start.3
  55.8 3.7 %copy-start.1 = (bf16[32,1,1,16,128]{0,1,4,3,2:T(2,128)(2,1)S(1)}, bf16[32,1,1,16,128]{0,1,4,3,2:T(2,128)(2,1)}, u32[]{:S(2)}) copy-start(bf16[32,1,1,16,128]{0,1,4,3,2:T(2,128)(2,1)} %copy.34) | copy-start | bytes 393220
  78.6 70.1 %reduce-scatter.2.cloned.1.call-start = ((), (), s32[]{:S(2)}) async-start(), calls=%async_computation.1 | async-start | bytes 655360 | tf_op jit(solution)/shard_map/reduce_scatter | solution.py:68
  87.0 0.7 copy-start.2
Sparse Core Ops, SparseCore 0:
  78.7 68.1 all-reduce.1
Sparse Core Ops, SparseCore 1:
  81.6 17.8 reduce-scatter.1
where the time goes:
time: 158 us
  waiting for transfers between devices  58.1 us (37%)
  blocking collectives  31.4 us (20%)
  matrix products  25.4 us (16%)
  local copies, waits for them, and re-layouts  15.7 us (10%)
  between operations  15.7 us (10%)
  starting transfers between devices  6.23 us (4%)
  other arithmetic  5.24 us (3%)
    psum x1, waiting for transfers between devices, on_device(): kernel_sum, bias_sum = lax.psum((kernel_local, bias_local), 'slab')  58 us
    psum x1, blocking collectives, on_device(): kernel_sum, bias_sum = lax.psum((kernel_local, bias_local), 'slab')  22.8 us
    transpose x1, matrix products, on_device(): kernel_local = jnp.transpose(correlate(gathered, out_grad), (2, 3, 4, 0, 1))  19.1 us
    all_gather x1, blocking collectives, on_device(): gathered = lax.all_gather(volume_rim, 'chan', axis=0, tiled=True)  8.63 us
    ppermute x1, starting transfers between devices, with_halo(): before = lax.ppermute(last, axis, up)  4.85 us
    conv_general_dilated x1, matrix products, conv_forward(): lax.conv_general_dilated(source[None], kernel, (1, 1, 1), ((depth_pad, de...  4.23 us
    unnamed x11, local copies, waits for them, and re-layouts  3.83 us
    broadcast_in_dim x1, local copies, waits for them, and re-layouts, correlate(): left[:, None]  3.67 us
  transfers between devices with their start and end apart: 4, of which 1 were waited for; matrix products, arithmetic and copies ran while one was open for 10% of the time, Pallas kernels for 0%

commit v1 on v0

v1 whole, which is shorter than its diff:
```python
import functools
import math

import jax
import jax.numpy as jnp
from jax import lax
from jax.experimental import pallas as pl
from jax.experimental.pallas import tpu as pltpu
from jax.sharding import PartitionSpec as P

F32 = jnp.float32
BF16 = jnp.bfloat16
MESH = pl.DeviceIdType.MESH


def roll_cols(value, step):
    width = value.shape[-1]
    lane = lax.broadcasted_iota(jnp.int32, value.shape, value.ndim - 1)
    edge = 0 if step > 0 else width - 1
    return jnp.where(lane == edge, 0.0, pltpu.roll(value, step % width, value.ndim - 1))


def body(slabs, chans, packed, scale, vol, ker, bias, og, feat, ig, kg, bg,
         tmp, rv, rg, xv3, xg3, vc, w1, w2, igs, igr, part, rs_s, rs_r, ag_r,
         v_send, v_recv, vh_send, g_send, g_recv, ig_send, ig_recv,
         rs_send, rs_recv, ag_send, ag_recv):
    c_in, o_loc = ker.shape[3], ker.shape[4]
    c_loc, rows, cols = vol.shape[0], vol.shape[2], vol.shape[3]
    cells = rows * cols
    s = lax.axis_index("slab")
    c = lax.axis_index("chan")
    has_prev, has_next = s > 0, s < slabs - 1

    def to_slab(t):
        return {"slab": t}

    def to_chan(t):
        return {"chan": t}

    peers = [lax.rem(c + k, chans) for k in range(1, chans)]
    others = [lax.rem(s + k, slabs) for k in range(1, slabs)] if packed else []

    barrier = pltpu.get_barrier_semaphore()
    for p in peers:
        pl.semaphore_signal(barrier, inc=1, device_id=to_chan(p), device_id_type=MESH)
    if packed:
        for t in others:
            pl.semaphore_signal(barrier, inc=1, device_id=to_slab(t), device_id_type=MESH)
    else:
        @pl.when(has_prev)
        def _():
            pl.semaphore_signal(barrier, inc=1, device_id=to_slab(s - 1), device_id_type=MESH)

        @pl.when(has_next)
        def _():
            pl.semaphore_signal(barrier, inc=1, device_id=to_slab(s + 1), device_id_type=MESH)

    tmp[...] = og[:, 0].astype(F32)
    for h in range(rows):
        rg[1, :, h * cols:(h + 1) * cols] = tmp[:, h, :].astype(BF16)
    tmp[:c_loc] = vol[:, 0].astype(F32)
    for h in range(rows):
        rv[1, c, :, h * cols:(h + 1) * cols] = tmp[:c_loc, h, :].astype(BF16)

    if packed:
        pl.semaphore_wait(barrier, chans - 1 + slabs - 1)
    else:
        pl.semaphore_wait(barrier, chans - 1)

        @pl.when(has_prev)
        def _():
            pl.semaphore_wait(barrier, 1)

        @pl.when(has_next)
        def _():
            pl.semaphore_wait(barrier, 1)

    def copy(src, dst, ssem, rsem, dev):
        return pltpu.make_async_remote_copy(
            src_ref=src, dst_ref=dst, send_sem=ssem, recv_sem=rsem,
            device_id=dev, device_id_type=MESH)

    g_up = copy(rg.at[1], rg.at[2], g_send.at[0], g_recv.at[2], to_slab(s + 1))
    g_down = copy(rg.at[1], rg.at[0], g_send.at[1], g_recv.at[0], to_slab(s - 1))
    v_up = copy(rv.at[1, c], rv.at[0, c], vh_send.at[0], v_recv.at[0, c], to_slab(s + 1))
    v_down = copy(rv.at[1, c], rv.at[2, c], vh_send.at[1], v_recv.at[2, c], to_slab(s - 1))

    def v_chan(a, p):
        return copy(rv.at[a, c], rv.at[a, c], v_send.at[a, p], v_recv.at[a, c], to_chan(p))

    def v_from(a, q):
        return copy(rv.at[a, q], rv.at[a, q], v_send.at[a, q], v_recv.at[a, q], to_chan(q))

    own_v = [v_chan(1, p) for p in peers]
    for d in own_v:
        d.start()

    @pl.when(has_next)
    def _():
        g_up.start()
        v_up.start()

    @pl.when(has_prev)
    def _():
        g_down.start()
        v_down.start()

    for cc in range(3):
        w2[cc * c_in:(cc + 1) * c_in, :] = jnp.concatenate(
            [ker[a, 2 - j, cc].astype(F32) for j in range(3) for a in range(3)], axis=1
        ).astype(BF16)
    wt = jnp.concatenate(
        [jnp.concatenate([ker[a, b, cc].astype(F32) for cc in range(3)], axis=1)
         for b in range(3) for a in range(3)], axis=0)
    w1[...] = jnp.transpose(wt).astype(BF16)

    def windows(dst, a, block):
        n = block.shape[0]
        zero = jnp.zeros((n, cols), BF16)
        for j in range(3):
            at = j * 3 * n + a * n
            if j == 1:
                dst[at:at + n, :] = block
            elif j == 0:
                dst[at:at + n, 0:cols] = zero
                dst[at:at + n, cols:cells] = block[:, 0:cells - cols]
            else:
                dst[at:at + n, 0:cells - cols] = block[:, cols:cells]
                dst[at:at + n, cells - cols:cells] = zero

    windows(xg3, 1, rg[1])
    vc[3 * c_in:, :] = jnp.ones((16, cells), BF16)

    for q in peers:
        v_from(1, q).wait_recv()
    v_own = jnp.concatenate([rv[1, q] for q in range(chans)], axis=0)
    windows(xv3, 1, v_own)
    for h in range(rows):
        block = v_own[:, h * cols:(h + 1) * cols]
        wide = block.astype(F32)
        at = slice(h * cols, (h + 1) * cols)
        vc[0:c_in, at] = roll_cols(wide, 1).astype(BF16)
        vc[c_in:2 * c_in, at] = block
        vc[2 * c_in:3 * c_in, at] = roll_cols(wide, -1).astype(BF16)

    @pl.when(has_next)
    def _():
        g_down.wait_recv()

    @pl.when(jnp.logical_not(has_next))
    def _():
        rg[0] = jnp.zeros((o_loc, cells), BF16)

    windows(xg3, 0, rg[0])

    @pl.when(has_prev)
    def _():
        g_up.wait_recv()

    @pl.when(jnp.logical_not(has_prev))
    def _():
        rg[2] = jnp.zeros((o_loc, cells), BF16)

    windows(xg3, 2, rg[2])

    part[:, 0:9 * o_loc] = lax.dot_general(
        vc[...], xg3[...], (((1,), (1,)), ((), ())), preferred_element_type=F32)
    if packed:
        ones_sum = part[3 * c_in:3 * c_in + 8, 4 * o_loc:5 * o_loc]
        for t in range(slabs):
            for r in range(3):
                at = 24 * t + 8 * r
                rs_s[t, 2 * r] = part[at:at + 8, 0:128]
                rs_s[t, 2 * r + 1] = part[at:at + 8, 128:256]
            rs_s[t, 6] = jnp.concatenate(
                [part[24 * t + 8 * r:24 * t + 8 * r + 8, 256:288] for r in range(3)]
                + [ones_sum], axis=1)
        rs_out = [copy(rs_s.at[t], rs_r.at[s], rs_send.at[t], rs_recv.at[s], to_slab(t))
                  for t in others]
        for d in rs_out:
            d.start()

    @pl.when(has_prev)
    def _():
        v_up.wait_recv()
        for p in peers:
            v_chan(0, p).start()

    @pl.when(has_next)
    def _():
        v_down.wait_recv()
        for p in peers:
            v_chan(2, p).start()

    share = jnp.dot(w2[...], xg3[...], preferred_element_type=F32)
    for h in range(rows):
        at = slice(h * cols, (h + 1) * cols)
        total = (share[c_in:2 * c_in, at] + roll_cols(share[0:c_in, at], -1)
                 + roll_cols(share[2 * c_in:3 * c_in, at], 1))
        for p in range(chans):
            igs[p, :, at] = total[p * c_loc:(p + 1) * c_loc]
    ig_out = [copy(igs.at[p], igr.at[c], ig_send.at[p], ig_recv.at[c], to_chan(p)) for p in peers]
    for d in ig_out:
        d.start()

    if packed:
        rs_r[s] = rs_s[s]
        for t in others:
            copy(rs_s.at[t], rs_r.at[t], rs_send.at[t], rs_recv.at[t], to_slab(t)).wait_recv()
        done = rs_r[0]
        for t in range(1, slabs):
            done = done + rs_r[t]
        done = done * scale
        ag_r[s] = done
        bg[...] = done[6, 0:1, 3 * o_loc:4 * o_loc]
        ag_out = [copy(ag_r.at[s], ag_r.at[s], ag_send.at[t], ag_recv.at[s], to_slab(t))
                  for t in others]
        for d in ag_out:
            d.start()
    else:
        bg[...] = part[3 * c_in:3 * c_in + 1, 4 * o_loc:5 * o_loc]
        for cc in range(3):
            for a in range(3):
                for b in range(3):
                    m = (2 - b) * 3 + a
                    kg[a, b, cc] = part[cc * c_in:(cc + 1) * c_in, m * o_loc:(m + 1) * o_loc]

    for a, here in ((0, has_prev), (2, has_next)):
        @pl.when(here)
        def _():
            for q in peers:
                v_from(a, q).wait_recv()

        @pl.when(jnp.logical_not(here))
        def _():
            rv[a] = jnp.zeros((chans, c_loc, cells), BF16)

        windows(xv3, a, jnp.concatenate([rv[a, q] for q in range(chans)], axis=0))
    pre = jnp.dot(w1[...], xv3[...], preferred_element_type=F32)
    bias_col = jnp.transpose(jnp.broadcast_to(bias[...], (cols, o_loc)))
    for h in range(rows):
        at = slice(h * cols, (h + 1) * cols)
        tmp[:, h, :] = (pre[o_loc:2 * o_loc, at] + roll_cols(pre[0:o_loc, at], 1)
                        + roll_cols(pre[2 * o_loc:3 * o_loc, at], -1) + bias_col)
    feat[:, 0] = tmp[...].astype(BF16)

    igr[c] = igs[c]
    for q in peers:
        copy(igs.at[q], igr.at[q], ig_send.at[q], ig_recv.at[q], to_chan(q)).wait_recv()
    for h in range(rows):
        at = slice(h * cols, (h + 1) * cols)
        total = igr[0, :, at]
        for q in range(1, chans):
            total = total + igr[q, :, at]
        tmp[:c_loc, h, :] = total
    ig[:, 0] = tmp[:c_loc].astype(BF16)

    if packed:
        for t in others:
            copy(ag_r.at[t], ag_r.at[t], ag_send.at[t], ag_recv.at[t], to_slab(t)).wait_recv()
        for t in range(slabs):
            for r in range(3):
                row = 24 * t + 8 * r
                cc, i = row // c_in, row % c_in
                for a in range(3):
                    for b in range(3):
                        m = (2 - b) * 3 + a
                        if m < 8:
                            k, lane = 2 * r + m // 4, (m % 4) * 32
                        else:
                            k, lane = 6, 32 * r
                        kg[a, b, cc, i:i + 8, :] = ag_r[t, k, :, lane:lane + 32]

    for d in own_v:
        d.wait_send()

    @pl.when(has_next)
    def _():
        g_up.wait_send()
        v_up.wait_send()
        for p in peers:
            v_chan(2, p).wait_send()

    @pl.when(has_prev)
    def _():
        g_down.wait_send()
        v_down.wait_send()
        for p in peers:
            v_chan(0, p).wait_send()

    for d in ig_out:
        d.wait_send()
    if packed:
        for d in rs_out + ag_out:
            d.wait_send()


def on_device(slabs, chans, volume, kernel, bias, out_grad):
    c_loc, _, rows, cols = volume.shape
    c_in, o_loc = kernel.shape[3], kernel.shape[4]
    cells = rows * cols
    packed = o_loc == 32 and 3 * c_in == 24 * slabs
    scale = 1.0 / math.sqrt(slabs * cells)
    vmem = pl.BlockSpec(memory_space=pltpu.VMEM)
    lanes = -(-9 * o_loc // 128) * 128
    parts = slabs if packed else 1
    dma = pltpu.SemaphoreType.DMA
    feature, input_grad, kernel_grad, bias_grad = pl.pallas_call(
        functools.partial(body, slabs, chans, packed, scale),
        out_shape=(
            jax.ShapeDtypeStruct((o_loc, 1, rows, cols), BF16),
            jax.ShapeDtypeStruct((c_loc, 1, rows, cols), BF16),
            jax.ShapeDtypeStruct(kernel.shape, F32),
            jax.ShapeDtypeStruct((1, o_loc), F32),
        ),
        in_specs=[vmem] * 4,
        out_specs=(vmem,) * 4,
        scratch_shapes=[
            pltpu.VMEM((max(o_loc, c_loc), rows, cols), F32),
            pltpu.VMEM((3, chans, c_loc, cells), BF16),
            pltpu.VMEM((3, o_loc, cells), BF16),
            pltpu.VMEM((9 * c_in, cells), BF16),
            pltpu.VMEM((9 * o_loc, cells), BF16),
            pltpu.VMEM((3 * c_in + 16, cells), BF16),
            pltpu.VMEM((3 * o_loc, 9 * c_in), BF16),
            pltpu.VMEM((3 * c_in, 9 * o_loc), BF16),
            pltpu.VMEM((chans, c_loc, cells), F32),
            pltpu.VMEM((chans, c_loc, cells), F32),
            pltpu.VMEM((3 * c_in + 16, lanes), F32),
            pltpu.VMEM((parts, 7, 8, 128), F32),
            pltpu.VMEM((parts, 7, 8, 128), F32),
            pltpu.VMEM((parts, 7, 8, 128), F32),
            dma((3, chans)), dma((3, chans)), dma((2,)), dma((2,)), dma((3,)),
            dma((chans,)), dma((chans,)),
            dma((parts,)), dma((parts,)), dma((parts,)), dma((parts,)),
        ],
        compiler_params=pltpu.CompilerParams(
            collective_id=0, has_side_effects=True, vmem_limit_bytes=40 * 1024 * 1024),
        cost_estimate=pl.CostEstimate(
            flops=3 * 2 * cells * 27 * c_in * o_loc, bytes_accessed=2 * 1024 * 1024,
            transcendentals=0),
    )(volume, kernel, bias.reshape(1, o_loc), out_grad)
    bias_grad = bias_grad.reshape(o_loc)
    if not packed:
        kernel_grad, bias_grad = lax.psum((kernel_grad, bias_grad), "slab")
        kernel_grad, bias_grad = kernel_grad * scale, bias_grad * scale
    return feature, input_grad, kernel_grad, bias_grad


def solution(mesh):
    specs = (
        P("chan", "slab", None, None),
        P(None, None, None, None, "chan"),
        P("chan"),
        P("chan", "slab", None, None),
    )
    out_specs = (specs[0], specs[0], specs[1], specs[2])
    run = functools.partial(on_device, mesh.shape["slab"], mesh.shape["chan"])
    return jax.shard_map(run, mesh=mesh, in_specs=specs, out_specs=out_specs, check_vma=False)
```

time: 158 us -> 33.5 us (0.21)
  the two profiles are of different devices: /device:TPU:0 before, /device:TPU:3 now
where the time goes in v1:
time: 33.5 us; the launch traced here: 33.4 us
  Pallas kernels  28.6 us (85%)
  local copies, waits for them, and re-layouts  4.08 us (12%)
  between operations  0.69 us (2%)
    pallas_call x1, Pallas kernels, on_device(): pl.pallas_call(functools.partial(body, slabs, chans, packed, scale), out_...  28.6 us
    unnamed x11, local copies, waits for them, and re-layouts  4.08 us

profile of v1, /device:TPU:3, one launch (start us, length us, event | category | flops | bytes accessed | tf_op | source)
XLA Modules:
  0.0 33.4 jit_solution(16724028205078702237)
XLA Ops:
  0.6 0.0 copy-start
  0.6 0.0 copy-start.1
  0.7 0.0 copy-start.2
  0.7 1.2 %copy.8.ker = bf16[3,3,3,64,32]{4,3,2,1,0:T(8,128)(2,1)S(1)} copy(bf16[3,3,3,64,32]{3,4,2,1,0:T(8,128)(2,1)} %param.5) | data formatting | bytes 221184 | tf_op args[1]
  1.9 0.0 copy-done
  1.9 0.0 copy-done.1
  1.9 0.0 copy-done.2
  1.9 28.6 %shard_map.75 = (bf16[32,1,16,128]{3,2,1,0:T(8,128)(2,1)S(1)}, bf16[16,1,16,128]{3,2,1,0:T(8,128)(2,1)S(1)}, f32[3,3,3,64,32]{4,3,2,1,0:T(8,128)S(1)}, f32[1,32]{1,0:T(1,128)S(1)}) custom-call(bf16[16,1,16,128]{3,2,1,0:T(8,128)(2,1)S(1)} %copy-done.1, bf16[3,3,3,64,32]{4,3,2,1,0:T(8,128)(2,1)S(1)} %copy.8.ker, f32[1,32]{1,0:T(1,128)S(1)} %bitcast.2, ...), custom_call_target="tpu_custom_call" | custom-call | flops 679477248 | bytes 2097152 | tf_op jit(solution)/shard_map/pallas_call | solution.py:308
  30.5 1.1 %copy.9 = f32[3,3,3,64,32]{3,4,2,1,0:T(8,128)} copy(f32[3,3,3,64,32]{4,3,2,1,0:T(8,128)S(1)} %get-tuple-element.14) | data formatting | bytes 442368
  31.6 0.7 %copy.13 = bf16[32,1,16,128]{3,2,1,0:T(8,128)(2,1)} copy(bf16[32,1,16,128]{3,2,1,0:T(8,128)(2,1)S(1)} %get-tuple-element.20) | data formatting | bytes 262144
  32.2 0.6 %copy.14 = bf16[16,1,16,128]{3,2,1,0:T(8,128)(2,1)} copy(bf16[16,1,16,128]{3,2,1,0:T(8,128)(2,1)S(1)} %get-tuple-element.21) | data formatting | bytes 131072
  32.9 0.5 %copy.15 = f32[32]{0:T(128)} copy(f32[32]{0:T(128)S(1)} %bitcast.3) | data formatting | bytes 256
Async XLA Ops:
  0.6 1.3 %copy-start = (bf16[32,1,16,128]{3,2,1,0:T(8,128)(2,1)S(1)}, bf16[32,1,16,128]{3,2,1,0:T(8,128)(2,1)}, u32[]{:S(2)}) copy-start(bf16[32,1,16,128]{3,2,1,0:T(8,128)(2,1)} %og.1) | copy-start | bytes 393220
  0.6 1.3 %copy-start.1 = (bf16[16,1,16,128]{3,2,1,0:T(8,128)(2,1)S(1)}, bf16[16,1,16,128]{3,2,1,0:T(8,128)(2,1)}, u32[]{:S(2)}) copy-start(bf16[16,1,16,128]{3,2,1,0:T(8,128)(2,1)} %vol.1) | copy-start | bytes 196612
  0.7 1.3 %copy-start.2 = (f32[32]{0:T(128)S(1)}, f32[32]{0:T(128)}, u32[]{:S(2)}) copy-start(f32[32]{0:T(128)} %param.6) | copy-start | bytes 388

commit v2 on v1

v2 whole, which is shorter than its diff:
```python
import functools
import math

import jax
import jax.numpy as jnp
from jax import lax
from jax.experimental import pallas as pl
from jax.experimental.pallas import tpu as pltpu
from jax.sharding import PartitionSpec as P

F32 = jnp.float32
BF16 = jnp.bfloat16
MESH = pl.DeviceIdType.MESH


def roll_cols(value, step):
    width = value.shape[-1]
    lane = lax.broadcasted_iota(jnp.int32, value.shape, value.ndim - 1)
    edge = 0 if step > 0 else width - 1
    return jnp.where(lane == edge, 0.0, pltpu.roll(value, step % width, value.ndim - 1))


def body(slabs, chans, packed, scale, vol, ker, bias, og, feat, ig, kg, bg,
         tmp, rv, rg, xv3, xg3, vc, w1, w2, igs, igr, part,
         s1, r1, a1, s2, r2, a2,
         v_send, v_recv, vh_send, g_send, g_recv, ig_send, ig_recv,
         s1_send, s1_recv, a1_send, a1_recv, s2_send, s2_recv, a2_send, a2_recv):
    o_loc, c_in = ker.shape[3], ker.shape[4]
    c_loc, rows, cols = vol.shape[0], vol.shape[2], vol.shape[3]
    cells = rows * cols
    s = lax.axis_index("slab")
    c = lax.axis_index("chan")
    has_prev, has_next = s > 0, s < slabs - 1

    def to_slab(t):
        return {"slab": t}

    def to_chan(t):
        return {"chan": t}

    def other_core(q):
        return q + 1 - 2 * lax.rem(q, 2)

    peers = [lax.rem(c + k, chans) for k in range(1, chans)]
    sib = other_core(c)
    same = [lax.rem(c + 2 * k, chans) for k in range(1, chans // 2)]
    others = [lax.rem(s + k, slabs) for k in range(1, slabs)] if packed else []

    barrier = pltpu.get_barrier_semaphore()
    for p in peers:
        pl.semaphore_signal(barrier, inc=1, device_id=to_chan(p), device_id_type=MESH)
    if packed:
        for t in others:
            pl.semaphore_signal(barrier, inc=1, device_id=to_slab(t), device_id_type=MESH)
    else:
        @pl.when(has_prev)
        def _():
            pl.semaphore_signal(barrier, inc=1, device_id=to_slab(s - 1), device_id_type=MESH)

        @pl.when(has_next)
        def _():
            pl.semaphore_signal(barrier, inc=1, device_id=to_slab(s + 1), device_id_type=MESH)

    tmp[...] = og[:, 0].astype(F32)
    for h in range(rows):
        rg[1, :, h * cols:(h + 1) * cols] = tmp[:, h, :].astype(BF16)
    tmp[:c_loc] = vol[:, 0].astype(F32)
    for h in range(rows):
        rv[1, c, :, h * cols:(h + 1) * cols] = tmp[:c_loc, h, :].astype(BF16)

    if packed:
        pl.semaphore_wait(barrier, chans - 1 + slabs - 1)
    else:
        pl.semaphore_wait(barrier, chans - 1)

        @pl.when(has_prev)
        def _():
            pl.semaphore_wait(barrier, 1)

        @pl.when(has_next)
        def _():
            pl.semaphore_wait(barrier, 1)

    def copy(src, dst, ssem, rsem, dev):
        return pltpu.make_async_remote_copy(
            src_ref=src, dst_ref=dst, send_sem=ssem, recv_sem=rsem,
            device_id=dev, device_id_type=MESH)

    g_up = copy(rg.at[1], rg.at[2], g_send.at[0], g_recv.at[2], to_slab(s + 1))
    g_down = copy(rg.at[1], rg.at[0], g_send.at[1], g_recv.at[0], to_slab(s - 1))
    v_up = copy(rv.at[1, c], rv.at[0, c], vh_send.at[0], v_recv.at[0, c], to_slab(s + 1))
    v_down = copy(rv.at[1, c], rv.at[2, c], vh_send.at[1], v_recv.at[2, c], to_slab(s - 1))

    def v_block(a, q, p, slot):
        return copy(rv.at[a, q], rv.at[a, q], v_send.at[a, slot], v_recv.at[a, q], to_chan(p))

    def v_first(a):
        return [v_block(a, c, p, p) for p in same] + [v_block(a, c, sib, sib)]

    def v_relay(a):
        return [v_block(a, q, sib, other_core(q)) for q in same]

    def v_relay_wait(a):
        for q, d in zip(same, v_relay(a)):
            v_block(a, q, sib, other_core(q)).wait_recv()
            d.start()

    def v_rest_wait(a):
        for q in [sib] + [other_core(q) for q in same]:
            v_block(a, q, sib, q).wait_recv()

    for d in v_first(1):
        d.start()

    @pl.when(has_next)
    def _():
        g_up.start()

    @pl.when(has_prev)
    def _():
        g_down.start()

    order = (0, 2, 1)
    w2t = jnp.concatenate(
        [jnp.concatenate([ker[a, 2 - j, cc].astype(F32) for cc in range(3)], axis=1)
         for a in order for j in range(3)], axis=0)
    w2[...] = jnp.transpose(w2t).astype(BF16)
    for cc in range(3):
        w1[cc * o_loc:(cc + 1) * o_loc, :] = jnp.concatenate(
            [ker[a, b, cc].astype(F32) for a in range(3) for b in range(3)], axis=1
        ).astype(BF16)

    def windows(dst, base, block):
        n = block.shape[0]
        zero = jnp.zeros((n, cols), BF16)
        at = base * 3 * n
        dst[at:at + n, 0:cols] = zero
        dst[at:at + n, cols:cells] = block[:, 0:cells - cols]
        dst[at + n:at + 2 * n, :] = block
        dst[at + 2 * n:at + 3 * n, 0:cells - cols] = block[:, cols:cells]
        dst[at + 2 * n:at + 3 * n, cells - cols:cells] = zero

    windows(xg3, 2, rg[1])
    nt = (((1,), (1,)), ((), ()))
    bias_part = lax.dot_general(
        jnp.ones((8, cells), BF16), rg[1], nt, preferred_element_type=F32)

    v_relay_wait(1)
    v_rest_wait(1)
    v_own = jnp.concatenate([rv[1, q] for q in range(chans)], axis=0)
    for h in range(rows):
        at = slice(h * cols, (h + 1) * cols)
        block = v_own[:, at]
        wide = block.astype(F32)
        vc[0:c_in, at] = roll_cols(wide, 1).astype(BF16)
        vc[c_in:2 * c_in, at] = block
        vc[2 * c_in:3 * c_in, at] = roll_cols(wide, -1).astype(BF16)

    half = 6 * o_loc
    wide_to = 3 * c_in
    part[half:, 0:wide_to] = lax.dot_general(
        xg3[half:, :], vc[...], nt, preferred_element_type=F32)

    def tiles(start, count):
        found = [part[start + 8 * k:start + 8 * k + 8, 0:128] for k in range(count)]
        for k in range(0, count, 2):
            found.append(jnp.concatenate(
                [part[start + 8 * k:start + 8 * k + 8, 128:192],
                 part[start + 8 * k + 8:start + 8 * k + 16, 128:192]], axis=1))
        return found

    def fill(dst, found):
        per = dst.shape[1]
        found = found + [jnp.zeros((8, 128), F32)] * (per * slabs - len(found))
        for k, tile in enumerate(found):
            dst[k // per, k % per] = tile

    def rs_copy(src, dst, ssem, rsem, t):
        return copy(src.at[t], dst.at[s], ssem.at[t], rsem.at[s], to_slab(t))

    def rs_from(src, dst, ssem, rsem, t):
        return copy(src.at[t], dst.at[t], ssem.at[t], rsem.at[t], to_slab(t))

    def ag_copy(buf, ssem, rsem, t):
        return copy(buf.at[s], buf.at[s], ssem.at[t], rsem.at[s], to_slab(t))

    def ag_from(buf, ssem, rsem, t):
        return copy(buf.at[t], buf.at[t], ssem.at[t], rsem.at[t], to_slab(t))

    def reduce_rows(src, dst, buf, ssem, rsem):
        dst[s] = src[s]
        for t in others:
            rs_from(src, dst, ssem, rsem, t).wait_recv()
        done = dst[0]
        for t in range(1, slabs):
            done = done + dst[t]
        buf[s] = done * scale

    if packed:
        fill(s1, tiles(half, 3 * o_loc // 8)
             + [jnp.concatenate([bias_part, jnp.zeros((8, 128 - o_loc), F32)], axis=1)])
        for t in others:
            rs_copy(s1, r1, s1_send, s1_recv, t).start()

    @pl.when(has_next)
    def _():
        v_up.start()

    @pl.when(has_prev)
    def _():
        v_down.start()

    @pl.when(has_next)
    def _():
        g_down.wait_recv()

    @pl.when(jnp.logical_not(has_next))
    def _():
        rg[0] = jnp.zeros((o_loc, cells), BF16)

    windows(xg3, 0, rg[0])

    @pl.when(has_prev)
    def _():
        g_up.wait_recv()

    @pl.when(jnp.logical_not(has_prev))
    def _():
        rg[2] = jnp.zeros((o_loc, cells), BF16)

    windows(xg3, 1, rg[2])
    part[0:half, 0:wide_to] = lax.dot_general(
        xg3[0:half, :], vc[...], nt, preferred_element_type=F32)
    if packed:
        fill(s2, tiles(0, half // 8))
        for t in others:
            rs_copy(s2, r2, s2_send, s2_recv, t).start()
        reduce_rows(s1, r1, a1, s1_send, s1_recv)
        for t in others:
            ag_copy(a1, a1_send, a1_recv, t).start()

    @pl.when(has_prev)
    def _():
        v_up.wait_recv()
        for d in v_first(0):
            d.start()

    @pl.when(has_next)
    def _():
        v_down.wait_recv()
        for d in v_first(2):
            d.start()

    share = jnp.dot(w2[...], xg3[...], preferred_element_type=F32)
    for h in range(rows):
        at = slice(h * cols, (h + 1) * cols)
        total = (share[c_in:2 * c_in, at] + roll_cols(share[0:c_in, at], -1)
                 + roll_cols(share[2 * c_in:3 * c_in, at], 1))
        for p in range(chans):
            igs[p, :, at] = total[p * c_loc:(p + 1) * c_loc]
    ig_out = [copy(igs.at[p], igr.at[c], ig_send.at[p], ig_recv.at[c], to_chan(p)) for p in peers]
    for d in ig_out:
        d.start()

    @pl.when(has_prev)
    def _():
        v_relay_wait(0)

    @pl.when(has_next)
    def _():
        v_relay_wait(2)

    if packed:
        reduce_rows(s2, r2, a2, s2_send, s2_recv)
        for t in others:
            ag_copy(a2, a2_send, a2_recv, t).start()
    else:
        bg[...] = bias_part[0:1, :]
        for k, a in enumerate(order):
            for j in range(3):
                for cc in range(3):
                    at = (k * 3 + j) * o_loc
                    kg[a, 2 - j, cc] = part[at:at + o_loc, cc * c_in:(cc + 1) * c_in]

    windows(xv3, 1, v_own)
    for a, here in ((0, has_prev), (2, has_next)):
        @pl.when(here)
        def _():
            v_rest_wait(a)

        @pl.when(jnp.logical_not(here))
        def _():
            rv[a] = jnp.zeros((chans, c_loc, cells), BF16)

        windows(xv3, a, jnp.concatenate([rv[a, q] for q in range(chans)], axis=0))
    pre = jnp.dot(w1[...], xv3[...], preferred_element_type=F32)
    bias_col = jnp.transpose(jnp.broadcast_to(bias[...], (cols, o_loc)))
    for h in range(rows):
        at = slice(h * cols, (h + 1) * cols)
        tmp[:, h, :] = (pre[o_loc:2 * o_loc, at] + roll_cols(pre[0:o_loc, at], 1)
                        + roll_cols(pre[2 * o_loc:3 * o_loc, at], -1) + bias_col)
    feat[:, 0] = tmp[...].astype(BF16)

    igr[c] = igs[c]
    for q in peers:
        copy(igs.at[q], igr.at[q], ig_send.at[q], ig_recv.at[q], to_chan(q)).wait_recv()
    for h in range(rows):
        at = slice(h * cols, (h + 1) * cols)
        total = igr[0, :, at]
        for q in range(1, chans):
            total = total + igr[q, :, at]
        tmp[:c_loc, h, :] = total
    ig[:, 0] = tmp[:c_loc].astype(BF16)

    def spread(buf, count, taps):
        per = buf.shape[1]
        for k in range(count):
            a, j, o = taps[k * 8 // (3 * o_loc)], (k * 8 // o_loc) % 3, k * 8 % o_loc
            m = count + k // 2
            low = buf[k // per, k % per]
            kg[a, 2 - j, 0, o:o + 8, :] = low[:, 0:c_in]
            kg[a, 2 - j, 1, o:o + 8, :] = low[:, c_in:2 * c_in]
            at = (k % 2) * c_in
            kg[a, 2 - j, 2, o:o + 8, :] = buf[m // per, m % per, :, at:at + c_in]

    if packed:
        for t in others:
            ag_from(a1, a1_send, a1_recv, t).wait_recv()
        spread(a1, 3 * o_loc // 8, (1,))
        k = (3 * o_loc // 8) * 3 // 2
        bg[...] = a1[k // a1.shape[1], k % a1.shape[1], 0:1, 0:o_loc]
        for t in others:
            ag_from(a2, a2_send, a2_recv, t).wait_recv()
        spread(a2, half // 8, (0, 2))

    for d in v_first(1) + v_relay(1):
        d.wait_send()

    @pl.when(has_next)
    def _():
        g_up.wait_send()
        v_up.wait_send()
        for d in v_first(2) + v_relay(2):
            d.wait_send()

    @pl.when(has_prev)
    def _():
        g_down.wait_send()
        v_down.wait_send()
        for d in v_first(0) + v_relay(0):
            d.wait_send()

    for d in ig_out:
        d.wait_send()
    for t in others:
        rs_copy(s1, r1, s1_send, s1_recv, t).wait_send()
        ag_copy(a1, a1_send, a1_recv, t).wait_send()
        rs_copy(s2, r2, s2_send, s2_recv, t).wait_send()
        ag_copy(a2, a2_send, a2_recv, t).wait_send()


def hand_out(feat, ig, kg, bg, feat_o, ig_o, kg_o, bg_o, sems):
    moves = [pltpu.make_async_copy(src, dst, sems.at[k]) for k, (src, dst) in enumerate(
        ((kg, kg_o), (feat, feat_o), (ig, ig_o), (bg, bg_o)))]
    for move in moves:
        move.start()
    for move in moves:
        move.wait()


def on_device(slabs, chans, volume, kernel, bias, out_grad):
    c_loc, _, rows, cols = volume.shape
    c_in, o_loc = kernel.shape[3], kernel.shape[4]
    cells = rows * cols
    packed = o_loc == 32 and c_in == 64 and slabs == 8
    scale = 1.0 / math.sqrt(slabs * cells)
    vmem = pl.BlockSpec(memory_space=pltpu.VMEM)
    parts = slabs if packed else 1
    dma = pltpu.SemaphoreType.DMA
    shapes = (
        jax.ShapeDtypeStruct((o_loc, 1, rows, cols), BF16),
        jax.ShapeDtypeStruct((c_loc, 1, rows, cols), BF16),
        jax.ShapeDtypeStruct((3, 3, 3, o_loc, c_in), F32),
        jax.ShapeDtypeStruct((1, o_loc), F32),
    )
    results = pl.pallas_call(
        functools.partial(body, slabs, chans, packed, scale),
        out_shape=shapes,
        in_specs=[vmem] * 4,
        out_specs=(vmem,) * 4,
        scratch_shapes=[
            pltpu.VMEM((max(o_loc, c_loc), rows, cols), F32),
            pltpu.VMEM((3, chans, c_loc, cells), BF16),
            pltpu.VMEM((3, o_loc, cells), BF16),
            pltpu.VMEM((9 * c_in, cells), BF16),
            pltpu.VMEM((9 * o_loc, cells), BF16),
            pltpu.VMEM((3 * c_in, cells), BF16),
            pltpu.VMEM((3 * o_loc, 9 * c_in), BF16),
            pltpu.VMEM((3 * c_in, 9 * o_loc), BF16),
            pltpu.VMEM((chans, c_loc, cells), F32),
            pltpu.VMEM((chans, c_loc, cells), F32),
            pltpu.VMEM((9 * o_loc, 256), F32),
        ] + [pltpu.VMEM((parts, 3, 8, 128), F32)] * 3 + [pltpu.VMEM((parts, 5, 8, 128), F32)] * 3
        + [dma((3, chans)), dma((3, chans)), dma((2,)), dma((2,)), dma((3,)),
           dma((chans,)), dma((chans,))] + [dma((parts,))] * 8,
        compiler_params=pltpu.CompilerParams(
            collective_id=0, has_side_effects=True, vmem_limit_bytes=40 * 1024 * 1024),
        cost_estimate=pl.CostEstimate(
            flops=3 * 2 * cells * 27 * c_in * o_loc, bytes_accessed=2 * 1024 * 1024,
            transcendentals=0),
    )(volume, jnp.swapaxes(kernel, 3, 4), bias.reshape(1, o_loc), out_grad)
    feature, input_grad, kernel_grad, bias_grad = pl.pallas_call(
        hand_out,
        out_shape=shapes,
        in_specs=[vmem] * 4,
        out_specs=(pl.BlockSpec(memory_space=pl.ANY),) * 4,
        scratch_shapes=[dma((4,))],
        compiler_params=pltpu.CompilerParams(vmem_limit_bytes=8 * 1024 * 1024),
        cost_estimate=pl.CostEstimate(flops=0, bytes_accessed=1024 * 1024, transcendentals=0),
    )(*results)
    bias_grad = bias_grad.reshape(o_loc)
    kernel_grad = jnp.swapaxes(kernel_grad, 3, 4)
    if not packed:
        kernel_grad, bias_grad = lax.psum((kernel_grad, bias_grad), "slab")
        kernel_grad, bias_grad = kernel_grad * scale, bias_grad * scale
    return feature, input_grad, kernel_grad, bias_grad


def solution(mesh):
    specs = (
        P("chan", "slab", None, None),
        P(None, None, None, None, "chan"),
        P("chan"),
        P("chan", "slab", None, None),
    )
    out_specs = (specs[0], specs[0], specs[1], specs[2])
    run = functools.partial(on_device, mesh.shape["slab"], mesh.shape["chan"])
    return jax.shard_map(run, mesh=mesh, in_specs=specs, out_specs=out_specs, check_vma=False)
```

time: 33.5 us -> 33.3 us (level)
  the two profiles are of different devices: /device:TPU:3 before, /device:TPU:0 now
where the time goes in v2:
time: 33.3 us; the launch traced here: 33.1 us
  Pallas kernels  29.1 us (87%)
  local copies, waits for them, and re-layouts  3.33 us (10%)
  between operations  0.65 us (2%)
    pallas_call x1, Pallas kernels, on_device(): pl.pallas_call(functools.partial(body, slabs, chans, packed, scale), out_...  28.2 us
    unnamed x8, local copies, waits for them, and re-layouts  3.33 us
    pallas_call x1, Pallas kernels, on_device(): pl.pallas_call(hand_out, out_shape=shapes, in_specs=[vmem] * 4, out_specs...  0.86 us

profile of v2, /device:TPU:0, one launch (start us, length us, event | category | flops | bytes accessed | tf_op | source)
XLA Modules:
  0.0 33.1 jit_solution(15834827791546489770)
XLA Ops:
  0.6 0.0 copy-start.3
  0.6 0.6 %copy-done.3 = f32[32]{0:T(128)S(1)} copy-done((f32[32]{0:T(128)S(1)}, f32[32]{0:T(128)}, u32[]{:S(2)}) %copy-start.3) | copy-done | bytes 152
  1.3 0.0 copy-start
  1.3 0.9 %copy-done = bf16[3,3,3,64,32]{3,4,2,1,0:T(8,128)(2,1)S(1)} copy-done((bf16[3,3,3,64,32]{3,4,2,1,0:T(8,128)(2,1)S(1)}, bf16[3,3,3,64,32]{3,4,2,1,0:T(8,128)(2,1)}, u32[]{:S(2)}) %copy-start) | copy-done | bytes 110616
  2.2 0.0 copy-start.1
  2.2 0.9 %copy-done.1 = bf16[32,1,16,128]{3,2,1,0:T(8,128)(2,1)S(1)} copy-done((bf16[32,1,16,128]{3,2,1,0:T(8,128)(2,1)S(1)}, bf16[32,1,16,128]{3,2,1,0:T(8,128)(2,1)}, u32[]{:S(2)}) %copy-start.1) | copy-done | bytes 131096
  3.1 0.0 copy-start.2
  3.1 0.8 %copy-done.2 = bf16[16,1,16,128]{3,2,1,0:T(8,128)(2,1)S(1)} copy-done((bf16[16,1,16,128]{3,2,1,0:T(8,128)(2,1)S(1)}, bf16[16,1,16,128]{3,2,1,0:T(8,128)(2,1)}, u32[]{:S(2)}) %copy-start.2) | copy-done | bytes 65560
  4.0 28.2 %shard_map.75 = (bf16[32,1,16,128]{3,2,1,0:T(8,128)(2,1)S(1)}, bf16[16,1,16,128]{3,2,1,0:T(8,128)(2,1)S(1)}, f32[3,3,3,32,64]{4,3,2,1,0:T(8,128)S(1)}, f32[1,32]{1,0:T(1,128)S(1)}) custom-call(bf16[16,1,16,128]{3,2,1,0:T(8,128)(2,1)S(1)} %copy-done.2, bf16[3,3,3,32,64]{4,3,2,1,0:T(8,128)(2,1)S(1)} %bitcast.4, f32[1,32]{1,0:T(1,128)S(1)} %bitcast.5, ...), custom_call_target="tpu_custom_call" | custom-call | flops 679477248 | bytes 2097152 | tf_op jit(solution)/shard_map/pallas_call | solution.py:386
  32.2 0.9 %shard_map.76 = (bf16[32,1,16,128]{3,2,1,0:T(8,128)(2,1)}, bf16[16,1,16,128]{3,2,1,0:T(8,128)(2,1)}, f32[3,3,3,32,64]{4,3,2,1,0:T(8,128)}, f32[1,32]{1,0:T(1,128)}) custom-call(bf16[32,1,16,128]{3,2,1,0:T(8,128)(2,1)S(1)} %get-tuple-element.12.feat, bf16[16,1,16,128]{3,2,1,0:T(8,128)(2,1)S(1)} %get-tuple-element.13.ig, ...), custom_call_target="tpu_custom_call" | custom-call | bytes 1048576 | tf_op jit(solution)/shard_map/pallas_call | solution.py:412
Async XLA Ops:
  0.6 0.7 %copy-start.3 = (f32[32]{0:T(128)S(1)}, f32[32]{0:T(128)}, u32[]{:S(2)}) copy-start(f32[32]{0:T(128)} %param.6) | copy-start | bytes 388
  1.3 0.9 %copy-start = (bf16[3,3,3,64,32]{3,4,2,1,0:T(8,128)(2,1)S(1)}, bf16[3,3,3,64,32]{3,4,2,1,0:T(8,128)(2,1)}, u32[]{:S(2)}) copy-start(bf16[3,3,3,64,32]{3,4,2,1,0:T(8,128)(2,1)} %param.5) | copy-start | bytes 331780
  2.2 0.9 %copy-start.1 = (bf16[32,1,16,128]{3,2,1,0:T(8,128)(2,1)S(1)}, bf16[32,1,16,128]{3,2,1,0:T(8,128)(2,1)}, u32[]{:S(2)}) copy-start(bf16[32,1,16,128]{3,2,1,0:T(8,128)(2,1)} %og.1) | copy-start | bytes 393220
  3.1 0.8 %copy-start.2 = (bf16[16,1,16,128]{3,2,1,0:T(8,128)(2,1)S(1)}, bf16[16,1,16,128]{3,2,1,0:T(8,128)(2,1)}, u32[]{:S(2)}) copy-start(bf16[16,1,16,128]{3,2,1,0:T(8,128)(2,1)} %vol.1) | copy-start | bytes 196612

commit v3 on v2

--- a/solution.py
+++ b/solution.py
@@ -20,8 +20,8 @@
     return jnp.where(lane == edge, 0.0, pltpu.roll(value, step % width, value.ndim - 1))
 
 
-def body(slabs, chans, packed, scale, vol, ker, bias, og, feat, ig, kg, bg,
-         tmp, rv, rg, xv3, xg3, vc, w1, w2, igs, igr, part,
+def body(slabs, chans, packed, scale, vol_in, ker_in, bias_in, og_in, feat, ig, kg, bg,
+         vol, ker, bias, og, in_sem, tmp, rv, rg, xv3, xg3, vc, w1, w2, igs, igr, part,
          s1, r1, a1, s2, r2, a2,
          v_send, v_recv, vh_send, g_send, g_recv, ig_send, ig_recv,
          s1_send, s1_recv, a1_send, a1_recv, s2_send, s2_recv, a2_send, a2_recv):
@@ -46,6 +46,11 @@
     same = [lax.rem(c + 2 * k, chans) for k in range(1, chans // 2)]
     others = [lax.rem(s + k, slabs) for k in range(1, slabs)] if packed else []
 
+    loads = [pltpu.make_async_copy(src, dst, in_sem.at[k]) for k, (src, dst) in enumerate(
+        ((og_in, og), (vol_in, vol), (ker_in, ker), (bias_in, bias)))]
+    for load in loads:
+        load.start()
+
     barrier = pltpu.get_barrier_semaphore()
     for p in peers:
         pl.semaphore_signal(barrier, inc=1, device_id=to_chan(p), device_id_type=MESH)
@@ -61,9 +66,11 @@
         def _():
             pl.semaphore_signal(barrier, inc=1, device_id=to_slab(s + 1), device_id_type=MESH)
 
+    loads[0].wait()
     tmp[...] = og[:, 0].astype(F32)
     for h in range(rows):
         rg[1, :, h * cols:(h + 1) * cols] = tmp[:, h, :].astype(BF16)
+    loads[1].wait()
     tmp[:c_loc] = vol[:, 0].astype(F32)
     for h in range(rows):
         rv[1, c, :, h * cols:(h + 1) * cols] = tmp[:c_loc, h, :].astype(BF16)
@@ -86,10 +93,39 @@
             src_ref=src, dst_ref=dst, send_sem=ssem, recv_sem=rsem,
             device_id=dev, device_id_type=MESH)
 
-    g_up = copy(rg.at[1], rg.at[2], g_send.at[0], g_recv.at[2], to_slab(s + 1))
-    g_down = copy(rg.at[1], rg.at[0], g_send.at[1], g_recv.at[0], to_slab(s - 1))
-    v_up = copy(rv.at[1, c], rv.at[0, c], vh_send.at[0], v_recv.at[0, c], to_slab(s + 1))
-    v_down = copy(rv.at[1, c], rv.at[2, c], vh_send.at[1], v_recv.at[2, c], to_slab(s - 1))
+    if packed:
+        x = lax.rem(s, 2)
+        near, far = 2 * x, 2 - 2 * x
+        has_near, pair = s >= 0, other_core(s)
+        has_far = jnp.logical_and(s + 2 * x >= 2, s + 2 * x < slabs)
+        relays = jnp.logical_and(s - 2 * x >= 0, s - 2 * x < slabs - 2)
+        g_near = [copy(rg.at[1, pl.ds(k, o_loc // 2)], rg.at[far, pl.ds(k, o_loc // 2)],
+                       g_send.at[0, i], g_recv.at[far, i], to_slab(pair))
+                  for i, k in enumerate((0, o_loc // 2))]
+        g_got = [copy(rg.at[1, pl.ds(k, o_loc // 2)], rg.at[near, pl.ds(k, o_loc // 2)],
+                      g_send.at[0, i], g_recv.at[near, i], to_slab(pair))
+                 for i, k in enumerate((0, o_loc // 2))]
+        g_far = [copy(rg.at[near, pl.ds(k, o_loc // 2)], rg.at[far, pl.ds(k, o_loc // 2)],
+                      g_send.at[1, i], g_recv.at[far, i], to_slab(s + 2 - 4 * x))
+                 for i, k in enumerate((0, o_loc // 2))]
+        vn, vf = far, near
+        v_near = copy(rv.at[1, c], rv.at[vf, c], vh_send.at[0], v_recv.at[vf, c], to_slab(pair))
+        v_got = copy(rv.at[1, c], rv.at[vn, c], vh_send.at[0], v_recv.at[vn, c], to_slab(pair))
+        v_far = copy(rv.at[vn, c], rv.at[vf, c], vh_send.at[1], v_recv.at[vf, c],
+                     to_slab(s + 2 - 4 * x))
+    else:
+        g_up = copy(rg.at[1], rg.at[2], g_send.at[0, 0], g_recv.at[2, 0], to_slab(s + 1))
+        g_down = copy(rg.at[1], rg.at[0], g_send.at[1, 0], g_recv.at[0, 0], to_slab(s - 1))
+        v_up = copy(rv.at[1, c], rv.at[0, c], vh_send.at[0], v_recv.at[0, c], to_slab(s + 1))
+        v_down = copy(rv.at[1, c], rv.at[2, c], vh_send.at[1], v_recv.at[2, c], to_slab(s - 1))
+
+    def relay_g(i):
+        if packed:
+            g_got[i].wait_recv()
+
+            @pl.when(relays)
+            def _():
+                g_far[i].start()
 
     def v_block(a, q, p, slot):
         return copy(rv.at[a, q], rv.at[a, q], v_send.at[a, slot], v_recv.at[a, q], to_chan(p))
@@ -112,14 +148,20 @@
     for d in v_first(1):
         d.start()
 
-    @pl.when(has_next)
-    def _():
-        g_up.start()
-
-    @pl.when(has_prev)
-    def _():
-        g_down.start()
-
+    if packed:
+        for d in g_near:
+            d.start()
+    else:
+        @pl.when(has_next)
+        def _():
+            g_up.start()
+
+        @pl.when(has_prev)
+        def _():
+            g_down.start()
+
+    loads[2].wait()
+    loads[3].wait()
     order = (0, 2, 1)
     w2t = jnp.concatenate(
         [jnp.concatenate([ker[a, 2 - j, cc].astype(F32) for cc in range(3)], axis=1)
@@ -146,6 +188,7 @@
         jnp.ones((8, cells), BF16), rg[1], nt, preferred_element_type=F32)
 
     v_relay_wait(1)
+    relay_g(0)
     v_rest_wait(1)
     v_own = jnp.concatenate([rv[1, q] for q in range(chans)], axis=0)
     for h in range(rows):
@@ -156,6 +199,18 @@
         vc[c_in:2 * c_in, at] = block
         vc[2 * c_in:3 * c_in, at] = roll_cols(wide, -1).astype(BF16)
 
+    relay_g(1)
+    if packed:
+        v_near.start()
+    else:
+        @pl.when(has_next)
+        def _():
+            v_up.start()
+
+        @pl.when(has_prev)
+        def _():
+            v_down.start()
+
     half = 6 * o_loc
     wide_to = 3 * c_in
     part[half:, 0:wide_to] = lax.dot_general(
@@ -202,17 +257,19 @@
         for t in others:
             rs_copy(s1, r1, s1_send, s1_recv, t).start()
 
-    @pl.when(has_next)
-    def _():
-        v_up.start()
-
-    @pl.when(has_prev)
-    def _():
-        v_down.start()
-
-    @pl.when(has_next)
-    def _():
-        g_down.wait_recv()
+    if packed:
+        @pl.when(has_far)
+        def _():
+            for d in g_far:
+                d.wait_recv()
+    else:
+        @pl.when(has_next)
+        def _():
+            g_down.wait_recv()
+
+        @pl.when(has_prev)
+        def _():
+            g_up.wait_recv()
 
     @pl.when(jnp.logical_not(has_next))
     def _():
@@ -220,10 +277,6 @@
 
     windows(xg3, 0, rg[0])
 
-    @pl.when(has_prev)
-    def _():
-        g_up.wait_recv()
-
     @pl.when(jnp.logical_not(has_prev))
     def _():
         rg[2] = jnp.zeros((o_loc, cells), BF16)
@@ -235,21 +288,31 @@
         fill(s2, tiles(0, half // 8))
         for t in others:
             rs_copy(s2, r2, s2_send, s2_recv, t).start()
+
+    if packed:
+        v_got.wait_recv()
+
+        @pl.when(relays)
+        def _():
+            v_far.start()
+
+        for d in v_first(vn):
+            d.start()
         reduce_rows(s1, r1, a1, s1_send, s1_recv)
         for t in others:
             ag_copy(a1, a1_send, a1_recv, t).start()
-
-    @pl.when(has_prev)
-    def _():
-        v_up.wait_recv()
-        for d in v_first(0):
-            d.start()
-
-    @pl.when(has_next)
-    def _():
-        v_down.wait_recv()
-        for d in v_first(2):
-            d.start()
+    else:
+        @pl.when(has_prev)
+        def _():
+            v_up.wait_recv()
+            for d in v_first(0):
+                d.start()
+
+        @pl.when(has_next)
+        def _():
+            v_down.wait_recv()
+            for d in v_first(2):
+                d.start()
 
     share = jnp.dot(w2[...], xg3[...], preferred_element_type=F32)
     for h in range(rows):
@@ -262,18 +325,31 @@
     for d in ig_out:
         d.start()
 
-    @pl.when(has_prev)
-    def _():
-        v_relay_wait(0)
-
-    @pl.when(has_next)
-    def _():
-        v_relay_wait(2)
+    if packed:
+        @pl.when(has_far)
+        def _():
+            v_far.wait_recv()
+            for d in v_first(vf):
+                d.start()
+
+        v_relay_wait(vn)
+    else:
+        @pl.when(has_prev)
+        def _():
+            v_relay_wait(0)
+
+        @pl.when(has_next)
+        def _():
+            v_relay_wait(2)
 
     if packed:
         reduce_rows(s2, r2, a2, s2_send, s2_recv)
         for t in others:
             ag_copy(a2, a2_send, a2_recv, t).start()
+
+        @pl.when(has_far)
+        def _():
+            v_relay_wait(vf)
     else:
         bg[...] = bias_part[0:1, :]
         for k, a in enumerate(order):
@@ -336,17 +412,32 @@
     for d in v_first(1) + v_relay(1):
         d.wait_send()
 
+    if packed:
+        for d in g_near + [v_near]:
+            d.wait_send()
+
+        @pl.when(relays)
+        def _():
+            for d in g_far + [v_far]:
+                d.wait_send()
+    else:
+        @pl.when(has_next)
+        def _():
+            g_up.wait_send()
+            v_up.wait_send()
+
+        @pl.when(has_prev)
+        def _():
+            g_down.wait_send()
+            v_down.wait_send()
+
     @pl.when(has_next)
     def _():
-        g_up.wait_send()
-        v_up.wait_send()
         for d in v_first(2) + v_relay(2):
             d.wait_send()
 
     @pl.when(has_prev)
     def _():
-        g_down.wait_send()
-        v_down.wait_send()
         for d in v_first(0) + v_relay(0):
             d.wait_send()
 
@@ -386,9 +477,14 @@
     results = pl.pallas_call(
         functools.partial(body, slabs, chans, packed, scale),
         out_shape=shapes,
-        in_specs=[vmem] * 4,
+        in_specs=[pl.BlockSpec(memory_space=pltpu.HBM)] * 4,
         out_specs=(vmem,) * 4,
         scratch_shapes=[
+            pltpu.VMEM(volume.shape, BF16),
+            pltpu.VMEM((3, 3, 3, o_loc, c_in), BF16),
+            pltpu.VMEM((1, o_loc), F32),
+            pltpu.VMEM(out_grad.shape, BF16),
+            dma((4,)),
             pltpu.VMEM((max(o_loc, c_loc), rows, cols), F32),
             pltpu.VMEM((3, chans, c_loc, cells), BF16),
             pltpu.VMEM((3, o_loc, cells), BF16),
@@ -401,10 +497,10 @@
             pltpu.VMEM((chans, c_loc, cells), F32),
             pltpu.VMEM((9 * o_loc, 256), F32),
         ] + [pltpu.VMEM((parts, 3, 8, 128), F32)] * 3 + [pltpu.VMEM((parts, 5, 8, 128), F32)] * 3
-        + [dma((3, chans)), dma((3, chans)), dma((2,)), dma((2,)), dma((3,)),
+        + [dma((3, chans)), dma((3, chans)), dma((2,)), dma((2, 2)), dma((3, 2)),
            dma((chans,)), dma((chans,))] + [dma((parts,))] * 8,
         compiler_params=pltpu.CompilerParams(
-            collective_id=0, has_side_effects=True, vmem_limit_bytes=40 * 1024 * 1024),
+            collective_id=0, has_side_effects=True, vmem_limit_bytes=64 * 1024 * 1024),
         cost_estimate=pl.CostEstimate(
             flops=3 * 2 * cells * 27 * c_in * o_loc, bytes_accessed=2 * 1024 * 1024,
             transcendentals=0),
@@ -412,10 +508,10 @@
     feature, input_grad, kernel_grad, bias_grad = pl.pallas_call(
         hand_out,
         out_shape=shapes,
-        in_specs=[vmem] * 4,
+        in_specs=[pl.BlockSpec(memory_space=pl.ANY)] * 4,
         out_specs=(pl.BlockSpec(memory_space=pl.ANY),) * 4,
         scratch_shapes=[dma((4,))],
-        compiler_params=pltpu.CompilerParams(vmem_limit_bytes=8 * 1024 * 1024),
+        compiler_params=pltpu.CompilerParams(vmem_limit_bytes=64 * 1024 * 1024),
         cost_estimate=pl.CostEstimate(flops=0, bytes_accessed=1024 * 1024, transcendentals=0),
     )(*results)
     bias_grad = bias_grad.reshape(o_loc)

time: 33.3 us -> 51.8 us (1.56)
  Pallas kernels: 29.1 us -> 51 us
  local copies, waits for them, and re-layouts: 3.33 us -> 0 us
    pallas_call x1, Pallas kernels: 0.86 us -> 20.5 us  [on_device(): pl.pallas_call(hand_out, out_shape=shapes, in_specs=[pl.BlockSpec(memory_...]
    unnamed x8 -> x0, local copies, waits for them, and re-layouts: 3.33 us -> none
    pallas_call x1, Pallas kernels: 28.2 us -> 30.5 us  [on_device(): pl.pallas_call(functools.partial(body, slabs, chans, packed, scale), out_...]
where the time goes in v3:
time: 51.8 us; the launch traced here: 51.6 us
  Pallas kernels  51 us (98%)
  between operations  0.64 us (1%)
    pallas_call x1, Pallas kernels, on_device(): pl.pallas_call(functools.partial(body, slabs, chans, packed, scale), out_...  30.5 us
    pallas_call x1, Pallas kernels, on_device(): pl.pallas_call(hand_out, out_shape=shapes, in_specs=[pl.BlockSpec(memory_...  20.5 us

profile of v3, /device:TPU:0, one launch (start us, length us, event | category | flops | bytes accessed | tf_op | source)
XLA Modules:
  0.0 51.6 jit_solution(17307554525569975822)
XLA Ops:
  0.6 30.5 %shard_map.75 = (bf16[32,1,16,128]{3,2,1,0:T(8,128)(2,1)}, bf16[16,1,16,128]{3,2,1,0:T(8,128)(2,1)}, f32[3,3,3,32,64]{4,3,2,1,0:T(8,128)}, f32[1,32]{1,0:T(1,128)}) custom-call(bf16[16,1,16,128]{3,2,1,0:T(8,128)(2,1)} %vol_in.1, bf16[3,3,3,32,64]{4,3,2,1,0:T(8,128)(2,1)} %bitcast.5, f32[1,32]{1,0:T(1,128)} %bitcast.6, bf16[32,1,16,128]{3,2,1,0:T(8,128)(2,1)} %og_in.1), custom_call_target="tpu_custom_call" | custom-call | flops 679477248 | bytes 2097152 | tf_op jit(solution)/shard_map/pallas_call | solution.py:477
  31.1 20.5 %shard_map.76 = (bf16[32,1,16,128]{3,2,1,0:T(8,128)(2,1)}, bf16[16,1,16,128]{3,2,1,0:T(8,128)(2,1)}, f32[3,3,3,32,64]{4,3,2,1,0:T(8,128)}, f32[1,32]{1,0:T(1,128)}) custom-call(bf16[32,1,16,128]{3,2,1,0:T(8,128)(2,1)} %get-tuple-element.12.feat, bf16[16,1,16,128]{3,2,1,0:T(8,128)(2,1)} %get-tuple-element.13.ig, f32[3,3,3,32,64]{4,3,2,1,0:T(8,128)} %get-tuple-element.14.kg, ...), custom_call_target="tpu_custom_call" | custom-call | bytes 1048576 | tf_op jit(solution)/shard_map/pallas_call | solution.py:508

commit v4 on v3

--- a/solution.py
+++ b/solution.py
@@ -508,7 +508,7 @@
     feature, input_grad, kernel_grad, bias_grad = pl.pallas_call(
         hand_out,
         out_shape=shapes,
-        in_specs=[pl.BlockSpec(memory_space=pl.ANY)] * 4,
+        in_specs=[vmem] * 4,
         out_specs=(pl.BlockSpec(memory_space=pl.ANY),) * 4,
         scratch_shapes=[dma((4,))],
         compiler_params=pltpu.CompilerParams(vmem_limit_bytes=64 * 1024 * 1024),

time: 51.8 us -> 33.3 us (0.64)
  Pallas kernels: 51 us -> 32.5 us
    pallas_call x1, Pallas kernels: 20.5 us -> 1.97 us  [on_device(): pl.pallas_call(hand_out, out_shape=shapes, in_specs=[vmem] * 4, out_specs...]
where the time goes in v4:
time: 33.3 us; the launch traced here: 33.1 us
  Pallas kernels  32.5 us (98%)
  between operations  0.64 us (2%)
    pallas_call x1, Pallas kernels, on_device(): pl.pallas_call(functools.partial(body, slabs, chans, packed, scale), out_...  30.5 us
    pallas_call x1, Pallas kernels, on_device(): pl.pallas_call(hand_out, out_shape=shapes, in_specs=[vmem] * 4, out_specs...  1.97 us

profile of v4, /device:TPU:0, one launch (start us, length us, event | category | flops | bytes accessed | tf_op | source)
XLA Modules:
  0.0 33.1 jit_solution(18257571470943130672)
XLA Ops:
  0.6 30.5 %shard_map.75 = (bf16[32,1,16,128]{3,2,1,0:T(8,128)(2,1)}, bf16[16,1,16,128]{3,2,1,0:T(8,128)(2,1)}, f32[3,3,3,32,64]{4,3,2,1,0:T(8,128)}, f32[1,32]{1,0:T(1,128)}) custom-call(bf16[16,1,16,128]{3,2,1,0:T(8,128)(2,1)} %vol_in.1, bf16[3,3,3,32,64]{4,3,2,1,0:T(8,128)(2,1)} %bitcast.5, f32[1,32]{1,0:T(1,128)} %bitcast.6, bf16[32,1,16,128]{3,2,1,0:T(8,128)(2,1)} %og_in.1), custom_call_target="tpu_custom_call" | custom-call | flops 679477248 | bytes 2097152 | tf_op jit(solution)/shard_map/pallas_call | solution.py:477
  31.1 2.0 %shard_map.76 = (bf16[32,1,16,128]{3,2,1,0:T(8,128)(2,1)}, bf16[16,1,16,128]{3,2,1,0:T(8,128)(2,1)}, f32[3,3,3,32,64]{4,3,2,1,0:T(8,128)}, f32[1,32]{1,0:T(1,128)}) custom-call(bf16[32,1,16,128]{3,2,1,0:T(8,128)(2,1)} %get-tuple-element.12.feat, bf16[16,1,16,128]{3,2,1,0:T(8,128)(2,1)} %get-tuple-element.13.ig, f32[3,3,3,32,64]{4,3,2,1,0:T(8,128)} %get-tuple-element.14.kg, ...), custom_call_target="tpu_custom_call" | custom-call | bytes 1048576 | tf_op jit(solution)/shard_map/pallas_call | solution.py:508

commit v5 on v2

--- a/solution.py
+++ b/solution.py
@@ -25,7 +25,7 @@
          s1, r1, a1, s2, r2, a2,
          v_send, v_recv, vh_send, g_send, g_recv, ig_send, ig_recv,
          s1_send, s1_recv, a1_send, a1_recv, s2_send, s2_recv, a2_send, a2_recv):
-    o_loc, c_in = ker.shape[3], ker.shape[4]
+    c_in, o_loc = ker.shape[3], ker.shape[4]
     c_loc, rows, cols = vol.shape[0], vol.shape[2], vol.shape[3]
     cells = rows * cols
     s = lax.axis_index("slab")
@@ -121,14 +121,14 @@
         g_down.start()
 
     order = (0, 2, 1)
-    w2t = jnp.concatenate(
-        [jnp.concatenate([ker[a, 2 - j, cc].astype(F32) for cc in range(3)], axis=1)
-         for a in order for j in range(3)], axis=0)
-    w2[...] = jnp.transpose(w2t).astype(BF16)
     for cc in range(3):
-        w1[cc * o_loc:(cc + 1) * o_loc, :] = jnp.concatenate(
-            [ker[a, b, cc].astype(F32) for a in range(3) for b in range(3)], axis=1
+        w2[cc * c_in:(cc + 1) * c_in, :] = jnp.concatenate(
+            [ker[a, 2 - j, cc].astype(F32) for a in order for j in range(3)], axis=1
         ).astype(BF16)
+    w1t = jnp.concatenate(
+        [jnp.concatenate([ker[a, b, cc].astype(F32) for cc in range(3)], axis=1)
+         for a in range(3) for b in range(3)], axis=0)
+    w1[...] = jnp.transpose(w1t).astype(BF16)
 
     def windows(dst, base, block):
         n = block.shape[0]
@@ -408,7 +408,7 @@
         cost_estimate=pl.CostEstimate(
             flops=3 * 2 * cells * 27 * c_in * o_loc, bytes_accessed=2 * 1024 * 1024,
             transcendentals=0),
-    )(volume, jnp.swapaxes(kernel, 3, 4), bias.reshape(1, o_loc), out_grad)
+    )(volume, kernel, bias.reshape(1, o_loc), out_grad)
     feature, input_grad, kernel_grad, bias_grad = pl.pallas_call(
         hand_out,
         out_shape=shapes,

time: 33.3 us -> 31.3 us (0.940)
  local copies, waits for them, and re-layouts: 3.33 us -> 1.23 us
    unnamed x8 -> x7, local copies, waits for them, and re-layouts: 3.33 us -> 1.23 us
where the time goes in v5:
time: 31.3 us; the launch traced here: 31.1 us
  Pallas kernels  29.2 us (93%)
  local copies, waits for them, and re-layouts  1.23 us (4%)
  between operations  0.69 us (2%)
    pallas_call x1, Pallas kernels, on_device(): pl.pallas_call(functools.partial(body, slabs, chans, packed, scale), out_...  28.4 us
    unnamed x7, local copies, waits for them, and re-layouts  1.23 us
    pallas_call x1, Pallas kernels, on_device(): pl.pallas_call(hand_out, out_shape=shapes, in_specs=[vmem] * 4, out_specs...  0.86 us

profile of v5, /device:TPU:0, one launch (start us, length us, event | category | flops | bytes accessed | tf_op | source)
XLA Modules:
  0.0 31.1 jit_solution(16366112337378385444)
XLA Ops:
  0.6 0.0 copy-start
  0.6 0.0 copy-start.1
  0.7 0.0 copy-start.2
  0.7 1.2 %copy.8.ker = bf16[3,3,3,64,32]{4,3,2,1,0:T(8,128)(2,1)S(1)} copy(bf16[3,3,3,64,32]{3,4,2,1,0:T(8,128)(2,1)} %param.5) | data formatting | bytes 221184 | tf_op args[1]
  1.9 0.0 copy-done
  1.9 0.0 copy-done.1
  1.9 0.0 copy-done.2
  1.9 28.4 %shard_map.75 = (bf16[32,1,16,128]{3,2,1,0:T(8,128)(2,1)S(1)}, bf16[16,1,16,128]{3,2,1,0:T(8,128)(2,1)S(1)}, f32[3,3,3,32,64]{4,3,2,1,0:T(8,128)S(1)}, f32[1,32]{1,0:T(1,128)S(1)}) custom-call(bf16[16,1,16,128]{3,2,1,0:T(8,128)(2,1)S(1)} %copy-done.1, bf16[3,3,3,64,32]{4,3,2,1,0:T(8,128)(2,1)S(1)} %copy.8.ker, f32[1,32]{1,0:T(1,128)S(1)} %bitcast.3, ...), custom_call_target="tpu_custom_call" | custom-call | flops 679477248 | bytes 2097152 | tf_op jit(solution)/shard_map/pallas_call | solution.py:386
  30.3 0.9 %shard_map.76 = (bf16[32,1,16,128]{3,2,1,0:T(8,128)(2,1)}, bf16[16,1,16,128]{3,2,1,0:T(8,128)(2,1)}, f32[3,3,3,32,64]{4,3,2,1,0:T(8,128)}, f32[1,32]{1,0:T(1,128)}) custom-call(bf16[32,1,16,128]{3,2,1,0:T(8,128)(2,1)S(1)} %get-tuple-element.12.feat, bf16[16,1,16,128]{3,2,1,0:T(8,128)(2,1)S(1)} %get-tuple-element.13.ig, ...), custom_call_target="tpu_custom_call" | custom-call | bytes 1048576 | tf_op jit(solution)/shard_map/pallas_call | solution.py:412
Async XLA Ops:
  0.6 1.3 %copy-start = (bf16[32,1,16,128]{3,2,1,0:T(8,128)(2,1)S(1)}, bf16[32,1,16,128]{3,2,1,0:T(8,128)(2,1)}, u32[]{:S(2)}) copy-start(bf16[32,1,16,128]{3,2,1,0:T(8,128)(2,1)} %og.1) | copy-start | bytes 393220
  0.6 1.3 %copy-start.1 = (bf16[16,1,16,128]{3,2,1,0:T(8,128)(2,1)S(1)}, bf16[16,1,16,128]{3,2,1,0:T(8,128)(2,1)}, u32[]{:S(2)}) copy-start(bf16[16,1,16,128]{3,2,1,0:T(8,128)(2,1)} %vol.1) | copy-start | bytes 196612
  0.7 1.3 %copy-start.2 = (f32[32]{0:T(128)S(1)}, f32[32]{0:T(128)}, u32[]{:S(2)}) copy-start(f32[32]{0:T(128)} %param.6) | copy-start | bytes 388
